TPU v7x, 512 devices: a whole 4x8x8 slice. The times are simulated.
512 devices in a mesh: grp: 16 (over y, x_lo), blk: 32 (over z, x_hi, core).
Axes of the slice: x: 4 (x_hi: 2, x_lo: 2; x = x_hi * 2 + x_lo), y: 8, z: 8, core: 2. Of those that a mesh axis runs over, the one named last changes fastest.
Arguments:
- picture_vectors: bfloat16 [131072, 1152], P(('grp', 'blk')), may hold values from -0.1875 to 0.1875
- caption_vectors: bfloat16 [131072, 1152], P(('grp', 'blk')), may hold values from -0.1875 to 0.1875
- positive_partner: int32 [131072], P(('grp', 'blk')), may hold values from 0 to 131071, as said below
- inverse_warmth: float32 [1], replicated, may hold values from 20 to 60
- affine_offset: float32 [1], replicated, may hold values from -4 to -1
Outputs:
- image_grad: bfloat16 [131072, 1152], P(('grp', 'blk'))
- text_grad: bfloat16 [131072, 1152], P(('grp', 'blk'))
Inputs may be any that keep to these rules, and one draw needn't show every extreme that they name: positive_partner[i] names a text of image i's group whose block lies 0 to 7 blocks before image i's block, cyclically over the 32 blocks of the group.
All inputs are finite; a program needn't handle non-finite values.
Results may differ from a plain program's by a relative error of at most 0.0045.
Values may be sent and summed in bfloat16 or wider, within the bound.
A program may use at most 64 MiB of HBM per device.

v0:
```python
import jax
import jax.numpy as jnp
from jax import lax
from jax.sharding import PartitionSpec as P

HOPS = 8


def shifted(block, axis, distance):
    devices = range(lax.axis_size(axis))
    route = [((i - distance) % len(devices), i) for i in devices]
    return lax.ppermute(block, axis, route)


def on_device(picture_vectors, caption_vectors, positive_partner, inverse_warmth, affine_offset):
    similarity_multiplier = inverse_warmth[0]
    offset = affine_offset[0]
    span_extent = lax.axis_size("blk")
    position = lax.axis_index("blk")
    batch_start_entry = lax.axis_index("grp") * span_extent
    rows = caption_vectors.shape[0]
    column_count = jnp.arange(rows)
    image_acc = jnp.zeros(picture_vectors.shape, jnp.float32)
    text_acc = jnp.zeros(caption_vectors.shape, jnp.float32)
    current = caption_vectors
    for step in range(HOPS):
        if step > 0:
            current = shifted(current, "blk", 1)
            text_acc = shifted(text_acc, "blk", 1)
        owner = (position - step) % span_extent
        text_ids = (batch_start_entry + owner) * rows + column_count
        sign = jnp.where(positive_partner[:, None] == text_ids[None, :], 1.0, -1.0).astype(
            jnp.float32
        )
        logits = (
            similarity_multiplier
            * lax.dot_general(
                picture_vectors,
                current,
                (((1,), (1,)), ((), ())),
                preferred_element_type=jnp.float32,
            )
            + offset
        )
        coeff = (-sign * similarity_multiplier * jax.nn.sigmoid(-sign * logits)).astype(
            jnp.bfloat16
        )
        image_acc = image_acc + jnp.dot(coeff, current, preferred_element_type=jnp.float32)
        text_acc = text_acc + lax.dot_general(
            coeff, picture_vectors, (((0,), (0,)), ((), ())), preferred_element_type=jnp.float32
        )
    text_resident_block = shifted(text_acc.astype(jnp.bfloat16), "blk", -(HOPS - 1)).astype(
        text_acc.dtype
    )
    image_grad = image_acc.astype(jnp.bfloat16)
    text_grad = text_resident_block.astype(jnp.bfloat16)
    return (image_grad, text_grad)


def solution(mesh):
    return jax.shard_map(
        on_device,
        mesh=mesh,
        in_specs=(P(("grp", "blk"), None), P(("grp", "blk"), None), P(("grp", "blk")), P(), P()),
        out_specs=(P(("grp", "blk"), None), P(("grp", "blk"), None)),
        check_vma=False,
    )
```

profile of v0, /device:TPU:48, one launch (start us, length us, event | category | flops | bytes accessed | tf_op | source)
XLA Modules:
  0.0 232.8 jit_solution(11162321841236711552)
XLA Ops:
  2.0 1.5 fusion.57
  4.6 1.9 collective-permute-start.7
  6.5 5.0 %collective-permute-start = (bf16[256,1152]{1,0:T(8,128)(2,1)S(1)}, bf16[256,1152]{1,0:T(8,128)(2,1)}, u32[]{:S(2)}, u32[]{:S(2)}) collective-permute-start(bf16[256,1152]{1,0:T(8,128)(2,1)S(1)} %copy-done.1), channel_id=1, source_target_pairs={{31,0},{0,1},{1,2},{2,3},{3,4},{4,5},{5,6},{6,7},{7,8},{8,9},{9,10... | collective-permute-start | bytes 1769480 | tf_op jit(solution)/shard_map/ppermute | solution.py:12
  11.6 26.1 %collective-permute-done = bf16[256,1152]{1,0:T(8,128)(2,1)} collective-permute-done((bf16[256,1152]{1,0:T(8,128)(2,1)S(1)}, bf16[256,1152]{1,0:T(8,128)(2,1)}, u32[]{:S(2)}, u32[]{:S(2)}) %collective-permute-start) | collective-permute-done | bytes 589856 | tf_op jit(solution)/shard_map/ppermute | solution.py:12
  37.7 1.5 fusion.58
  39.9 1.9 collective-permute-start.8
  41.8 1.9 collective-permute-start.1
  43.7 23.7 %collective-permute-done.1 = bf16[256,1152]{1,0:T(8,128)(2,1)} collective-permute-done((bf16[256,1152]{1,0:T(8,128)(2,1)}, bf16[256,1152]{1,0:T(8,128)(2,1)}, u32[]{:S(2)}, u32[]{:S(2)}) %collective-permute-start.1) | collective-permute-done | bytes 589856 | tf_op jit(solution)/shard_map/ppermute | solution.py:12
  67.4 1.5 fusion.59
  69.7 1.9 collective-permute-start.9
  71.6 1.9 collective-permute-start.2
  73.6 23.7 %collective-permute-done.2 = bf16[256,1152]{1,0:T(8,128)(2,1)} collective-permute-done((bf16[256,1152]{1,0:T(8,128)(2,1)}, bf16[256,1152]{1,0:T(8,128)(2,1)}, u32[]{:S(2)}, u32[]{:S(2)}) %collective-permute-start.2) | collective-permute-done | bytes 589856 | tf_op jit(solution)/shard_map/ppermute | solution.py:12
  97.2 1.5 fusion.60
  99.5 1.9 collective-permute-start.10
  101.4 1.9 collective-permute-start.3
  103.4 23.7 %collective-permute-done.3 = bf16[256,1152]{1,0:T(8,128)(2,1)} collective-permute-done((bf16[256,1152]{1,0:T(8,128)(2,1)}, bf16[256,1152]{1,0:T(8,128)(2,1)}, u32[]{:S(2)}, u32[]{:S(2)}) %collective-permute-start.3) | collective-permute-done | bytes 589856 | tf_op jit(solution)/shard_map/ppermute | solution.py:12
  127.1 1.5 fusion.61
  129.3 1.9 collective-permute-start.11
  131.3 1.9 collective-permute-start.4
  133.3 23.6 %collective-permute-done.4 = bf16[256,1152]{1,0:T(8,128)(2,1)} collective-permute-done((bf16[256,1152]{1,0:T(8,128)(2,1)}, bf16[256,1152]{1,0:T(8,128)(2,1)}, u32[]{:S(2)}, u32[]{:S(2)}) %collective-permute-start.4) | collective-permute-done | bytes 589856 | tf_op jit(solution)/shard_map/ppermute | solution.py:12
  156.9 1.9 collective-permute-start.5
  158.8 1.5 fusion.62
  160.8 2.1 collective-permute-start.12
  163.3 1.4 convolution_add_fusion.7
  164.7 7.2 %collective-permute-done.5 = bf16[256,1152]{1,0:T(8,128)(2,1)S(1)} collective-permute-done((bf16[256,1152]{1,0:T(8,128)(2,1)}, bf16[256,1152]{1,0:T(8,128)(2,1)S(1)}, u32[]{:S(2)}, u32[]{:S(2)}) %collective-permute-start.5) | collective-permute-done | bytes 589856 | tf_op jit(solution)/shard_map/ppermute | solution.py:12
  172.7 11.8 %collective-permute-done.12 = f32[256,1152]{1,0:T(8,128)S(1)} collective-permute-done((f32[256,1152]{1,0:T(8,128)S(1)}, f32[256,1152]{1,0:T(8,128)S(1)}, u32[]{:S(2)}, u32[]{:S(2)}) %collective-permute-start.12) | collective-permute-done | bytes 1179680 | tf_op jit(solution)/shard_map/ppermute | solution.py:12
  184.7 2.1 collective-permute-start.13
  186.7 1.4 convolution_add_fusion.6
  188.2 2.1 collective-permute-start.6
  193.1 19.2 %collective-permute-done.6 = bf16[256,1152]{1,0:T(8,128)(2,1)S(1)} collective-permute-done((bf16[256,1152]{1,0:T(8,128)(2,1)S(1)}, bf16[256,1152]{1,0:T(8,128)(2,1)S(1)}, u32[]{:S(2)}, u32[]{:S(2)}) %collective-permute-start.6) | collective-permute-done | bytes 589856 | tf_op jit(solution)/shard_map/ppermute | solution.py:12
  213.2 1.9 collective-permute-start.14
  218.1 13.9 %collective-permute-done.14 = bf16[256,1152]{1,0:T(8,128)(2,1)S(1)} collective-permute-done((bf16[256,1152]{1,0:T(8,128)(2,1)S(1)}, bf16[256,1152]{1,0:T(8,128)(2,1)S(1)}, u32[]{:S(2)}, u32[]{:S(2)}) %collective-permute-start.14) | collective-permute-done | bytes 589856 | tf_op jit(solution)/shard_map/ppermute | solution.py:12
  (63 shorter events, 13.2 us)
Async XLA Ops:
  0.6 1.4 copy-start
  3.5 0.7 copy-start.10
  4.2 2.3 copy-start.1
  4.2 33.5 %copy-start.12 = (s32[256]{0:T(256)S(1)}, s32[256]{0:T(256)}, u32[]{:S(2)}) copy-start(s32[256]{0:T(256)} %param.7) | copy-start | bytes 3076
  4.6 34.6 %collective-permute-start.7 = (f32[256,1152]{1,0:T(8,128)S(1)}, f32[256,1152]{1,0:T(8,128)S(1)}, u32[]{:S(2)}, u32[]{:S(2)}) collective-permute-start(f32[256,1152]{1,0:T(8,128)S(1)} %fusion.66), channel_id=1, source_target_pairs={{31,0},{0,1},{1,2},{2,3},{3,4},{4,5},{5,6},{6,7},{7,8},{8,9},{9,10... | collective-permute-start | bytes 3538952 | tf_op jit(solution)/shard_map/ppermute | solution.py:12
  6.5 31.2 %collective-permute-start = (bf16[256,1152]{1,0:T(8,128)(2,1)S(1)}, bf16[256,1152]{1,0:T(8,128)(2,1)}, u32[]{:S(2)}, u32[]{:S(2)}) collective-permute-start(bf16[256,1152]{1,0:T(8,128)(2,1)S(1)} %copy-done.1), channel_id=1, source_target_pairs={{31,0},{0,1},{1,2},{2,3},{3,4},{4,5},{5,6},{6,7},{7,8},{8,9},{9,10... | collective-permute-start | bytes 1769480 | tf_op jit(solution)/shard_map/ppermute | solution.py:12
  39.2 0.7 copy-start.2
  39.9 29.7 %collective-permute-start.8 = (f32[256,1152]{1,0:T(8,128)S(1)}, f32[256,1152]{1,0:T(8,128)S(1)}, u32[]{:S(2)}, u32[]{:S(2)}) collective-permute-start(f32[256,1152]{1,0:T(8,128)S(1)} %convolution_add_fusion), channel_id=1, source_target_pairs={{31,0},{0,1},{1,2},{2,3},{3,4},{4,5},{5,6},{6,7},{7,8},{8,9},{9,10... | collective-permute-start | bytes 3538952 | tf_op jit(solution)/shard_map/ppermute | solution.py:12
  41.8 25.6 %collective-permute-start.1 = (bf16[256,1152]{1,0:T(8,128)(2,1)}, bf16[256,1152]{1,0:T(8,128)(2,1)}, u32[]{:S(2)}, u32[]{:S(2)}) collective-permute-start(bf16[256,1152]{1,0:T(8,128)(2,1)} %collective-permute-done), channel_id=1, source_target_pairs={{31,0},{0,1},{1,2},{2,3},{3,4},{4,5},{5,6},{6,7},{7,8},{8,9},{9,10... | collective-permute-start | bytes 1769480 | tf_op jit(solution)/shard_map/ppermute | solution.py:12
  68.9 0.7 copy-start.4
  69.7 29.7 %collective-permute-start.9 = (f32[256,1152]{1,0:T(8,128)S(1)}, f32[256,1152]{1,0:T(8,128)S(1)}, u32[]{:S(2)}, u32[]{:S(2)}) collective-permute-start(f32[256,1152]{1,0:T(8,128)S(1)} %add.293), channel_id=1, source_target_pairs={{31,0},{0,1},{1,2},{2,3},{3,4},{4,5},{5,6},{6,7},{7,8},{8,9},{9,10... | collective-permute-start | bytes 3538952 | tf_op jit(solution)/shard_map/ppermute | solution.py:12
  71.6 25.6 %collective-permute-start.2 = (bf16[256,1152]{1,0:T(8,128)(2,1)}, bf16[256,1152]{1,0:T(8,128)(2,1)}, u32[]{:S(2)}, u32[]{:S(2)}) collective-permute-start(bf16[256,1152]{1,0:T(8,128)(2,1)} %collective-permute-done.1), channel_id=1, source_target_pairs={{31,0},{0,1},{1,2},{2,3},{3,4},{4,5},{5,6},{6,7},{7,8},{8,9},{9,10... | collective-permute-start | bytes 1769480 | tf_op jit(solution)/shard_map/ppermute | solution.py:12
  98.7 0.6 copy-start.6
  99.5 29.7 %collective-permute-start.10 = (f32[256,1152]{1,0:T(8,128)S(1)}, f32[256,1152]{1,0:T(8,128)S(1)}, u32[]{:S(2)}, u32[]{:S(2)}) collective-permute-start(f32[256,1152]{1,0:T(8,128)S(1)} %add.294), channel_id=1, source_target_pairs={{31,0},{0,1},{1,2},{2,3},{3,4},{4,5},{5,6},{6,7},{7,8},{8,9},{9,10... | collective-permute-start | bytes 3538952 | tf_op jit(solution)/shard_map/ppermute | solution.py:12
  101.4 25.6 %collective-permute-start.3 = (bf16[256,1152]{1,0:T(8,128)(2,1)}, bf16[256,1152]{1,0:T(8,128)(2,1)}, u32[]{:S(2)}, u32[]{:S(2)}) collective-permute-start(bf16[256,1152]{1,0:T(8,128)(2,1)} %collective-permute-done.2), channel_id=1, source_target_pairs={{31,0},{0,1},{1,2},{2,3},{3,4},{4,5},{5,6},{6,7},{7,8},{8,9},{9,10... | collective-permute-start | bytes 1769480 | tf_op jit(solution)/shard_map/ppermute | solution.py:12
  128.6 0.6 copy-start.8
  129.3 31.4 %collective-permute-start.11 = (f32[256,1152]{1,0:T(8,128)S(1)}, f32[256,1152]{1,0:T(8,128)S(1)}, u32[]{:S(2)}, u32[]{:S(2)}) collective-permute-start(f32[256,1152]{1,0:T(8,128)S(1)} %add.295), channel_id=1, source_target_pairs={{31,0},{0,1},{1,2},{2,3},{3,4},{4,5},{5,6},{6,7},{7,8},{8,9},{9,10... | collective-permute-start | bytes 3538952 | tf_op jit(solution)/shard_map/ppermute | solution.py:12
  131.3 25.6 %collective-permute-start.4 = (bf16[256,1152]{1,0:T(8,128)(2,1)}, bf16[256,1152]{1,0:T(8,128)(2,1)}, u32[]{:S(2)}, u32[]{:S(2)}) collective-permute-start(bf16[256,1152]{1,0:T(8,128)(2,1)} %collective-permute-done.3), channel_id=1, source_target_pairs={{31,0},{0,1},{1,2},{2,3},{3,4},{4,5},{5,6},{6,7},{7,8},{8,9},{9,10... | collective-permute-start | bytes 1769480 | tf_op jit(solution)/shard_map/ppermute | solution.py:12
  156.9 15.0 %collective-permute-start.5 = (bf16[256,1152]{1,0:T(8,128)(2,1)}, bf16[256,1152]{1,0:T(8,128)(2,1)S(1)}, u32[]{:S(2)}, u32[]{:S(2)}) collective-permute-start(bf16[256,1152]{1,0:T(8,128)(2,1)} %collective-permute-done.4), channel_id=1, source_target_pairs={{31,0},{0,1},{1,2},{2,3},{3,4},{4,5},{5,6},{6,7},{7,8},{8,9},{9,10... | collective-permute-start | bytes 1769480 | tf_op jit(solution)/shard_map/ppermute | solution.py:12
  160.7 2.2 copy-start.11
  160.8 2.4 %copy-start.3 = (bf16[256,256]{1,0:T(8,128)(2,1)S(1)}, bf16[256,256]{1,0:T(8,128)(2,1)}, u32[]{:S(2)}) copy-start(bf16[256,256]{1,0:T(8,128)(2,1)} %copy-done.2) | copy-start | bytes 393220
  160.8 23.7 %collective-permute-start.12 = (f32[256,1152]{1,0:T(8,128)S(1)}, f32[256,1152]{1,0:T(8,128)S(1)}, u32[]{:S(2)}, u32[]{:S(2)}) collective-permute-start(f32[256,1152]{1,0:T(8,128)S(1)} %add.296), channel_id=1, source_target_pairs={{31,0},{0,1},{1,2},{2,3},{3,4},{4,5},{5,6},{6,7},{7,8},{8,9},{9,10... | collective-permute-start | bytes 3538952 | tf_op jit(solution)/shard_map/ppermute | solution.py:12
  172.7 14.0 %copy-start.5 = (bf16[256,256]{1,0:T(8,128)(2,1)S(1)}, bf16[256,256]{1,0:T(8,128)(2,1)}, u32[]{:S(2)}) copy-start(bf16[256,256]{1,0:T(8,128)(2,1)} %copy-done.4) | copy-start | bytes 393220
  184.7 5.6 %copy-start.7 = (bf16[256,256]{1,0:T(8,128)(2,1)S(1)}, bf16[256,256]{1,0:T(8,128)(2,1)}, u32[]{:S(2)}) copy-start(bf16[256,256]{1,0:T(8,128)(2,1)} %copy-done.6) | copy-start | bytes 393220
  184.7 28.4 %collective-permute-start.13 = (f32[256,1152]{1,0:T(8,128)S(1)}, f32[256,1152]{1,0:T(8,128)S(1)}, u32[]{:S(2)}, u32[]{:S(2)}) collective-permute-start(f32[256,1152]{1,0:T(8,128)S(1)} %add.297), channel_id=1, source_target_pairs={{31,0},{0,1},{1,2},{2,3},{3,4},{4,5},{5,6},{6,7},{7,8},{8,9},{9,10... | collective-permute-start | bytes 3538952 | tf_op jit(solution)/shard_map/ppermute | solution.py:12
  188.2 3.5 %copy-start.9 = (bf16[256,256]{1,0:T(8,128)(2,1)S(1)}, bf16[256,256]{1,0:T(8,128)(2,1)}, u32[]{:S(2)}) copy-start(bf16[256,256]{1,0:T(8,128)(2,1)} %copy-done.8) | copy-start | bytes 393220
  188.2 24.1 %collective-permute-start.6 = (bf16[256,1152]{1,0:T(8,128)(2,1)S(1)}, bf16[256,1152]{1,0:T(8,128)(2,1)S(1)}, u32[]{:S(2)}, u32[]{:S(2)}) collective-permute-start(bf16[256,1152]{1,0:T(8,128)(2,1)S(1)} %collective-permute-done.5), channel_id=1, source_target_pairs={{31,0},{0,1},{1,2},{2,3},{3,4},{4,5},{5,6},{6,7},{7,8},{8,9},{9,10... | collective-permute-start | bytes 1769480 | tf_op jit(solution)/shard_map/ppermute | solution.py:12
  213.2 18.8 %collective-permute-start.14 = (bf16[256,1152]{1,0:T(8,128)(2,1)S(1)}, bf16[256,1152]{1,0:T(8,128)(2,1)S(1)}, u32[]{:S(2)}, u32[]{:S(2)}) collective-permute-start(bf16[256,1152]{1,0:T(8,128)(2,1)S(1)} %add_convert_fusion), channel_id=1, source_target_pairs={{7,0},{8,1},{9,2},{10,3},{11,4},{12,5},{13,6},{14,7},{15,8},{16,9}... | collective-permute-start | bytes 1769480 | tf_op jit(solution)/shard_map/ppermute | solution.py:12
where the time goes:
time: 234 us; the launch traced here: 233 us
  waiting for transfers between devices  173 us (74%)
  starting transfers between devices  32.3 us (14%)
  matrix products  21.7 us (9%)
  between operations  2.65 us (1%)
  local copies, waits for them, and re-layouts  2.55 us (1%)
    ppermute x15, waiting for transfers between devices, shifted(): return lax.ppermute(block, axis, route)  173 us
    ppermute x15, starting transfers between devices, shifted(): return lax.ppermute(block, axis, route)  32.3 us
    dot_general x8, matrix products, on_device(): lax.dot_general(picture_vectors, current, (((1,), (1,)), ((), ())), prefe...  9.79 us
    dot_general x8, matrix products, on_device(): jnp.dot(coeff, current, preferred_element_type=jnp.float32)  8.9 us
  transfers between devices with their start and end apart: 15, of which 9 were waited for; matrix products, arithmetic and copies ran while one was open for 8% of the time, Pallas kernels for 0%

commit v1 on v0

v1 whole, which is shorter than its diff:
```python
import functools

import jax
import jax.numpy as jnp
from jax import lax
from jax.experimental import pallas as pl
from jax.experimental.pallas import tpu as pltpu
from jax.sharding import PartitionSpec as P

MESH = pl.DeviceIdType.MESH
HOPS = 8
CHUNKS = 4
TEXT, IMAGE = 0, 1


def kernel(
    n_blk, scale_ref, offset_ref, images, texts, labels, image_out, text_out,
    held, rows_of, column_of, total, stage, local_sem, recv, send, row_recv, row_send,
):
    rows = images.shape[0]
    part = rows // CHUNKS
    n_z = n_blk // 4
    group = lax.axis_index("grp")
    p = lax.axis_index("blk")
    z, x_hi, core = p // 4, (p // 2) % 2, p % 2
    sibling = {"blk": p + 1 - 2 * core}
    partner = {"blk": p + 2 - 4 * x_hi}
    early, late = 1 - x_hi, x_hi
    outer, inner = core, 1 - core

    def along(kind):
        step = 1 - 2 * kind
        return {"blk": lax.rem(z + step + n_z, n_z) * 4 + x_hi * 2 + core}

    loads = [
        pltpu.make_async_copy(texts, held.at[TEXT, 0], local_sem.at[0]),
        pltpu.make_async_copy(images, held.at[IMAGE, 0], local_sem.at[1]),
    ]
    for load in loads:
        load.start()
    barrier = pltpu.get_barrier_semaphore()
    for device in (sibling, partner, along(TEXT), along(IMAGE)):
        pl.semaphore_signal(barrier, inc=1, device_id=device, device_id_type=MESH)

    base = (group * n_blk + p) * rows
    rows_of[TEXT, 0] = base + lax.broadcasted_iota(jnp.int32, (1, rows), 1)
    rows_of[IMAGE, 0] = labels[...]
    column_of[TEXT] = jnp.transpose(jnp.broadcast_to(labels[...], (128, rows)))
    column_of[IMAGE] = base + lax.broadcasted_iota(jnp.int32, (rows, 128), 0)
    for load in loads:
        load.wait()
    pl.semaphore_wait(barrier, 4)

    def copy(route, kind, slot, chunk, to_slot, device):
        span = pl.ds(chunk * part, part)
        return pltpu.make_async_remote_copy(
            src_ref=held.at[kind, slot, span],
            dst_ref=held.at[kind, to_slot, span],
            send_sem=send.at[route, kind, slot, chunk],
            recv_sem=recv.at[kind, to_slot, chunk],
            device_id=device,
            device_id_type=MESH,
        )

    def row_copy(route, kind, slot, to_slot, device):
        return pltpu.make_async_remote_copy(
            src_ref=rows_of.at[kind, slot],
            dst_ref=rows_of.at[kind, to_slot],
            send_sem=row_send.at[route, kind, slot],
            recv_sem=row_recv.at[kind, to_slot],
            device_id=device,
            device_id_type=MESH,
        )

    def by_z(kind, slot, to_slot):
        return (0, kind, slot, to_slot, along(kind))

    def by_x(kind, slot):
        return (1, kind, slot, 2, partner)

    def by_core(kind, slot):
        return (2, kind, slot, slot + jnp.where(kind == outer, 1, -1), sibling)

    def put(transfer, chunk):
        route, kind, slot, to_slot, device = transfer
        copy(route, kind, slot, chunk, to_slot, device).start()
        if chunk == 0:
            row_copy(route, kind, slot, to_slot, device).start()

    def arrived(kind, slot, chunk):
        copy(0, kind, slot, chunk, slot, sibling).wait_recv()
        if chunk == 0:
            row_copy(0, kind, slot, slot, sibling).wait_recv()

    def arrived_whole(kind, slot):
        for chunk in range(CHUNKS):
            arrived(kind, slot, chunk)

    total[...] = jnp.zeros_like(total)
    for chunk in range(CHUNKS):
        put(by_z(early, 0, 4), chunk)
        put(by_z(late, 0, 4), chunk)
        put(by_x(late, 0), chunk)
    for chunk in range(CHUNKS):
        put(by_core(outer, 0), chunk)

    def first_wave(chunk):
        arrived(early, 4, chunk)
        put(by_x(early, 4), chunk)
        put(by_core(early, 4), chunk)
        arrived(late, 4, chunk)
        put(by_core(late, 4), chunk)
        arrived(early, 2, chunk)
        put(by_z(early, 2, 6), chunk)
        put(by_core(early, 2), chunk)
        arrived(outer, 3, chunk)
        put(by_z(outer, 3, 7), chunk)

    def second_wave(chunk):
        arrived(late, 2, chunk)
        put(by_z(late, 2, 6), chunk)
        put(by_core(late, 2), chunk)
        arrived(early, 6, chunk)
        put(by_core(early, 6), chunk)

    def last_wave(chunk):
        arrived(late, 6, chunk)
        put(by_core(late, 6), chunk)

    def odd(kind, outer_slot):
        return jnp.where(kind == outer, outer_slot, outer_slot + 2)

    order = [
        (early, 0), (late, 0), (inner, 1),
        (early, 2), (early, 4), (late, 4), (outer, 3), (inner, 5), (early, odd(early, 1)),
        (late, 2), (late, odd(late, 1)), (early, 6), (early, odd(early, 5)),
        (outer, 7), (late, 6), (late, odd(late, 5)),
    ]

    def before(n):
        if n == 2:
            arrived_whole(inner, 1)
        if n == 3:
            for chunk in range(CHUNKS):
                first_wave(chunk)
        if n == 7:
            second_wave(0)
            arrived_whole(inner, 5)
        if n == 8:
            second_wave(1)
            arrived_whole(*order[8])
        if n == 9:
            second_wave(2)
            last_wave(0)
            second_wave(3)
            last_wave(1)
        if n == 10:
            arrived_whole(*order[10])
        if n == 12:
            last_wave(2)
            arrived_whole(*order[12])
        if n == 13:
            last_wave(3)
            arrived_whole(*order[13])
        if n == 15:
            arrived_whole(*order[15])

    scale = scale_ref[0]
    offset = offset_ref[0]

    def unit(n, carry):
        for step in range(len(order)):
            pl.when(n == step)(functools.partial(before, step))
        kind, slot = order[0]
        for step in range(1, len(order)):
            kind = jnp.where(n == step, order[step][0], kind)
            slot = jnp.where(n == step, order[step][1], slot)
        block = held[kind, slot]
        logits = scale * lax.dot_general(
            held[1 - kind, 0], block, (((1,), (1,)), ((), ())), preferred_element_type=jnp.float32
        ) + offset
        column = jnp.concatenate([column_of[kind]] * (rows // 128), axis=1)
        turn = jnp.where(column == rows_of[kind, slot], -1.0, 1.0)
        coeff = (turn * scale * jax.nn.sigmoid(turn * logits)).astype(jnp.bfloat16)
        total[kind] += jnp.dot(coeff, block, preferred_element_type=jnp.float32)
        return carry

    lax.fori_loop(0, len(order), unit, 0)

    stage[...] = total[...].astype(jnp.bfloat16)
    stores = [
        pltpu.make_async_copy(stage.at[TEXT], image_out, local_sem.at[0]),
        pltpu.make_async_copy(stage.at[IMAGE], text_out, local_sem.at[1]),
    ]
    for store in stores:
        store.start()
    sent = [
        by_z(early, 0, 4), by_z(late, 0, 4), by_x(late, 0), by_core(outer, 0),
        by_x(early, 4), by_core(early, 4), by_core(late, 4),
        by_z(early, 2, 6), by_core(early, 2), by_z(outer, 3, 7),
        by_z(late, 2, 6), by_core(late, 2), by_core(early, 6), by_core(late, 6),
    ]
    for route, kind, slot, to_slot, device in sent:
        for chunk in range(CHUNKS):
            copy(route, kind, slot, chunk, to_slot, device).wait_send()
        row_copy(route, kind, slot, to_slot, device).wait_send()
    for store in stores:
        store.wait()


def solution(mesh):
    n_blk = mesh.shape["blk"]

    def on_device(picture_vectors, caption_vectors, positive_partner, inverse_warmth, affine_offset):
        rows, depth = picture_vectors.shape
        out = jax.ShapeDtypeStruct((rows, depth), jnp.bfloat16)
        whole = pl.BlockSpec(memory_space=pl.ANY)
        scalar = pl.BlockSpec(memory_space=pltpu.SMEM)
        return pl.pallas_call(
            functools.partial(kernel, n_blk),
            out_shape=(out, out),
            in_specs=[scalar, scalar, whole, whole, pl.BlockSpec(memory_space=pltpu.VMEM)],
            out_specs=(whole, whole),
            scratch_shapes=[
                pltpu.VMEM((2, HOPS, rows, depth), jnp.bfloat16),
                pltpu.VMEM((2, HOPS, 1, rows), jnp.int32),
                pltpu.VMEM((2, rows, 128), jnp.int32),
                pltpu.VMEM((2, rows, depth), jnp.float32),
                pltpu.VMEM((2, rows, depth), jnp.bfloat16),
                pltpu.SemaphoreType.DMA((2,)),
                pltpu.SemaphoreType.DMA((2, HOPS, CHUNKS)),
                pltpu.SemaphoreType.DMA((3, 2, HOPS, CHUNKS)),
                pltpu.SemaphoreType.DMA((2, HOPS)),
                pltpu.SemaphoreType.DMA((3, 2, HOPS)),
            ],
            compiler_params=pltpu.CompilerParams(
                collective_id=0, has_side_effects=True, vmem_limit_bytes=48 * 2**20
            ),
            cost_estimate=pl.CostEstimate(
                flops=64 * rows * rows * depth, bytes_accessed=8 * rows * depth, transcendentals=0
            ),
        )(inverse_warmth, affine_offset, picture_vectors, caption_vectors, positive_partner.reshape(1, rows))

    return jax.shard_map(
        on_device,
        mesh=mesh,
        in_specs=(P(("grp", "blk"), None), P(("grp", "blk"), None), P(("grp", "blk")), P(), P()),
        out_specs=(P(("grp", "blk"), None), P(("grp", "blk"), None)),
        check_vma=False,
    )
```

time: 234 us -> 60.2 us (0.26)
  the two profiles are of different devices: /device:TPU:48 before, /device:TPU:1 now
where the time goes in v1:
time: 60.2 us; the launch traced here: 60 us
  Pallas kernels  53.6 us (89%)
  local copies, waits for them, and re-layouts  4.43 us (7%)
  between operations  1.94 us (3%)
    pallas_call x1, Pallas kernels, on_device(): pl.pallas_call(functools.partial(kernel, n_blk), out_shape=(out, out), in...  53.6 us
    unnamed x8, local copies, waits for them, and re-layouts  4.43 us

profile of v1, /device:TPU:1, one launch (start us, length us, event | category | flops | bytes accessed | tf_op | source)
XLA Modules:
  0.0 60.0 jit_solution(14497041204703653643)
XLA Ops:
  1.9 0.0 copy-start.2
  1.9 0.7 %copy-done.2 = s32[256]{0:T(256)S(1)} copy-done((s32[256]{0:T(256)S(1)}, s32[256]{0:T(256)}, u32[]{:S(2)}) %copy-start.2) | copy-done | bytes 1048
  2.6 0.0 copy-start
  2.6 1.1 %copy-done = bf16[256,1152]{1,0:T(8,128)(2,1)S(1)} copy-done((bf16[256,1152]{1,0:T(8,128)(2,1)S(1)}, bf16[256,1152]{1,0:T(8,128)(2,1)}, u32[]{:S(2)}) %copy-start) | copy-done | bytes 589848
  3.7 0.0 copy-start.1
  3.7 1.1 %copy-done.1 = bf16[256,1152]{1,0:T(8,128)(2,1)S(1)} copy-done((bf16[256,1152]{1,0:T(8,128)(2,1)S(1)}, bf16[256,1152]{1,0:T(8,128)(2,1)}, u32[]{:S(2)}) %copy-start.1) | copy-done | bytes 589848
  4.7 53.6 %shard_map.68 = (bf16[256,1152]{1,0:T(8,128)(2,1)S(1)}, bf16[256,1152]{1,0:T(8,128)(2,1)S(1)}) custom-call(f32[1]{0:T(128)S(6)} %copy.9.scale_ref, f32[1]{0:T(128)S(6)} %copy.10.offset_ref, bf16[256,1152]{1,0:T(8,128)(2,1)S(1)} %copy-done, bf16[256,1152]{1,0:T(8,128)(2,1)S(1)} %copy-done.1, s32[1,256]{1,0:T(1,128)S(1)} %bitcast.1), custom_call_target="tpu_custom_call" | custom-call | flops 4831838208 | bytes 2359296 | tf_op jit(solution)/shard_map/pallas_call | solution.py:219
  58.3 0.8 %copy.11 = bf16[256,1152]{1,0:T(8,128)(2,1)} copy(bf16[256,1152]{1,0:T(8,128)(2,1)S(1)} %get-tuple-element.4) | data formatting | bytes 1179648
  59.2 0.8 %copy.12 = bf16[256,1152]{1,0:T(8,128)(2,1)} copy(bf16[256,1152]{1,0:T(8,128)(2,1)S(1)} %get-tuple-element.5) | data formatting | bytes 1179648
Async XLA Ops:
  1.9 0.7 %copy-start.2 = (s32[256]{0:T(256)S(1)}, s32[256]{0:T(256)}, u32[]{:S(2)}) copy-start(s32[256]{0:T(256)} %param.7) | copy-start | bytes 3076
  2.6 1.1 %copy-start = (bf16[256,1152]{1,0:T(8,128)(2,1)S(1)}, bf16[256,1152]{1,0:T(8,128)(2,1)}, u32[]{:S(2)}) copy-start(bf16[256,1152]{1,0:T(8,128)(2,1)} %images.1) | copy-start | bytes 1769476
  3.7 1.1 %copy-start.1 = (bf16[256,1152]{1,0:T(8,128)(2,1)S(1)}, bf16[256,1152]{1,0:T(8,128)(2,1)}, u32[]{:S(2)}) copy-start(bf16[256,1152]{1,0:T(8,128)(2,1)} %texts.1) | copy-start | bytes 1769476

commit v2 on v1

v2 whole, which is shorter than its diff:
```python
import functools

import jax
import jax.numpy as jnp
from jax import lax
from jax.experimental import pallas as pl
from jax.experimental.pallas import tpu as pltpu
from jax.sharding import PartitionSpec as P

MESH = pl.DeviceIdType.MESH
HOPS = 8
TEXT, IMAGE = 0, 1
VMEM_LIMIT = 40 * 2**20


def kernel(
    n_blk, scale_ref, offset_ref, images, texts, labels, image_out, text_out,
    held, rows_of, column_of, total, local_sem, recv, send, row_recv, row_send,
):
    rows = images.shape[0]
    half_rows, part = rows // 2, rows // 4
    n_z = n_blk // 4
    p = lax.axis_index("blk")
    z, x_hi, core = p // 4, (p // 2) % 2, p % 2
    sibling = {"blk": p + 1 - 2 * core}
    partner = {"blk": p + 2 - 4 * x_hi}
    early, late = 1 - x_hi, x_hi
    outer, inner = core, 1 - core
    up = lax.rem(z + 1, n_z) * 4 + p % 4
    down = lax.rem(z + n_z - 1, n_z) * 4 + p % 4

    def along(kind):
        return {"blk": jnp.where(kind == TEXT, up, down)}

    along_early, along_late, along_outer = along(early), along(late), along(outer)

    barrier = pltpu.get_barrier_semaphore()
    for device in (sibling, partner, along_early, along_late):
        pl.semaphore_signal(barrier, inc=1, device_id=device, device_id_type=MESH)
    loads = [
        pltpu.make_async_copy(texts, held.at[TEXT, 0], local_sem.at[0]),
        pltpu.make_async_copy(images, held.at[IMAGE, 0], local_sem.at[1]),
        pltpu.make_async_copy(labels, rows_of.at[IMAGE, 0], local_sem.at[2]),
    ]
    for load in loads:
        load.start()
    for load in loads:
        load.wait()
    pl.semaphore_wait(barrier, 4)

    def sem_of(kind, slot, q, is_odd):
        if is_odd:
            return recv.at[24 + kind * 8 + slot // 2 * 2 + q // 2]
        return recv.at[kind * 12 + (slot // 2 - 1) * 4 + q]

    def copy(kind, slot, q, n, to_slot, is_odd, device):
        span = pl.ds(q * part, n * part)
        return pltpu.make_async_remote_copy(
            src_ref=held.at[kind, slot, span],
            dst_ref=held.at[kind, to_slot, span],
            send_sem=send.at[0],
            recv_sem=sem_of(kind, to_slot, q - q % 2 if is_odd else q, is_odd),
            device_id=device,
            device_id_type=MESH,
        )

    def row_copy(slot, to_slot, device):
        return pltpu.make_async_remote_copy(
            src_ref=rows_of.at[IMAGE, slot],
            dst_ref=rows_of.at[IMAGE, to_slot],
            send_sem=row_send.at[0],
            recv_sem=row_recv.at[to_slot - 1],
            device_id=device,
            device_id_type=MESH,
        )

    def put(kind, slot, q, n, to_slot, is_odd, device):
        copy(kind, slot, q, n, to_slot, is_odd, device).start()
        if q == 0:
            @pl.when(kind == IMAGE)
            def _():
                row_copy(slot, to_slot, device).start()

    def by_z(kind, slot, q, n, to_slot, device):
        put(kind, slot, q, n, to_slot, to_slot == 7, device)

    def by_x(kind, slot, q, n):
        put(kind, slot, q, n, 2, False, partner)

    def by_core(kind, slot, q, n):
        put(kind, slot, q, n, slot + jnp.where(kind == outer, 1, -1), True, sibling)

    def arrived(kind, slot, q, n, is_odd=False):
        copy(kind, slot, q, n, slot, is_odd, sibling).wait_recv()
        if q == 0:
            @pl.when(kind == IMAGE)
            def _():
                row_copy(slot, slot, sibling).wait_recv()

    for q in range(4):
        by_z(early, 0, q, 1, 4, along_early)
        if q % 2 == 0:
            by_z(late, 0, q, 2, 4, along_late)
            by_x(late, 0, q, 2)
    by_core(outer, 0, 0, 4)

    base = lax.axis_index("grp") * n_blk * rows
    total[...] = jnp.zeros_like(total)
    column_of[IMAGE] = base + p * rows + lax.broadcasted_iota(jnp.int32, (rows, 128), 0)
    for half in range(2):
        column_of[TEXT, pl.ds(half * half_rows, half_rows)] = jnp.transpose(
            jnp.broadcast_to(rows_of[IMAGE, 0, half], (128, half_rows))
        )
        for slot in range(HOPS):
            block = lax.rem(p - slot + n_blk, n_blk)
            rows_of[TEXT, slot, half] = (
                base + block * rows + half * half_rows + lax.broadcasted_iota(jnp.int32, (1, half_rows), 1)
            )

    def first_wave(q):
        arrived(early, 4, q, 1)
        by_x(early, 4, q, 1)
        if q % 2 == 0:
            return
        by_core(early, 4, q - 1, 2)
        arrived(late, 4, q - 1, 2)
        by_core(late, 4, q - 1, 2)
        arrived(early, 2, q - 1, 2)
        by_z(early, 2, q - 1, 2, 6, along_early)
        arrived(outer, 3, q - 1, 2, True)
        by_z(outer, 3, q - 1, 2, 7, along_outer)

    def second_wave(q):
        arrived(late, 2, q, 1)
        by_z(late, 2, q, 1, 6, along_late)
        if q % 2 == 1:
            arrived(early, 6, q - 1, 2)

    def last_wave(q):
        arrived(late, 6, q, 1)
        if q == 1:
            by_core(late, 6, 0, 2)
        if q > 1:
            by_core(late, 6, q, 1)

    def odd(kind, outer_slot):
        return jnp.where(kind == outer, outer_slot, outer_slot + 2)

    def both(kind, slot):
        return (kind, slot, 0, slot, 1)

    order = [
        both(early, 0), both(late, 0), both(inner, 1),
        both(early, 2), both(early, 4), both(late, 4),
        both(outer, 3), both(inner, 5), both(early, odd(early, 1)),
        both(late, 2), both(late, odd(late, 1)), both(early, 6), both(early, odd(early, 5)),
        (late, 6, 0, odd(late, 5), 0), both(outer, 7), (late, 6, 1, odd(late, 5), 1),
    ]

    def before(n):
        if n == 2:
            arrived(inner, 1, 0, 4, True)
        if n == 3:
            for q in range(4):
                first_wave(q)
            by_core(early, 2, 0, 4)
        if n == 6:
            second_wave(0)
        if n == 7:
            arrived(inner, 5, 0, 2, True)
            arrived(inner, 5, 2, 2, True)
        if n == 8:
            second_wave(1)
            arrived(early, odd(early, 1), 0, 4, True)
        if n == 9:
            second_wave(2)
            last_wave(0)
            second_wave(3)
            by_core(late, 2, 0, 4)
            by_core(early, 6, 0, 4)
            last_wave(1)
        if n == 10:
            arrived(late, odd(late, 1), 0, 4, True)
        if n == 11:
            last_wave(2)
        if n == 12:
            arrived(early, odd(early, 5), 0, 4, True)
        if n == 13:
            last_wave(3)
            arrived(late, odd(late, 5), 0, 2, True)
        if n == 14:
            arrived(outer, 7, 0, 2, True)
            arrived(outer, 7, 2, 2, True)
        if n == 15:
            arrived(late, odd(late, 5), 2, 2, True)

    scale = scale_ref[0]
    offset = offset_ref[0]

    def unit(n, carry):
        for step in range(len(order)):
            pl.when(n == step)(functools.partial(before, step))
        picked = list(order[0])
        for step in range(1, len(order)):
            for i in range(len(picked)):
                picked[i] = jnp.where(n == step, order[step][i], picked[i])
        kind, slot_a, half_a, slot_b, half_b = picked

        def piece(slot, half):
            return held[kind, slot, pl.ds(pl.multiple_of(half * half_rows, half_rows), half_rows)]

        block = jnp.concatenate([piece(slot_a, half_a), piece(slot_b, half_b)], axis=0)
        line = jnp.concatenate([rows_of[kind, slot_a, half_a], rows_of[kind, slot_b, half_b]], axis=1)
        logits = scale * lax.dot_general(
            held[1 - kind, 0], block, (((1,), (1,)), ((), ())), preferred_element_type=jnp.float32
        ) + offset
        column = jnp.concatenate([column_of[kind]] * (rows // 128), axis=1)
        turn = jnp.where(column == line, -1.0, 1.0)
        coeff = (turn * scale * jax.nn.sigmoid(turn * logits)).astype(jnp.bfloat16)
        total[kind] += jnp.dot(coeff, block, preferred_element_type=jnp.float32)
        return carry

    lax.fori_loop(0, len(order), unit, 0)

    image_out[...] = total[TEXT].astype(jnp.bfloat16)
    text_out[...] = total[IMAGE].astype(jnp.bfloat16)
    blocks = held.at[:, pl.ds(0, HOPS - 1)]
    pltpu.make_async_remote_copy(
        blocks, blocks, send.at[0], recv.at[0], device_id=sibling, device_id_type=MESH
    ).wait_send()
    for kind, count in ((IMAGE, HOPS), (TEXT, HOPS - 2)):
        @pl.when(outer == kind)
        def _():
            lines = rows_of.at[IMAGE, pl.ds(0, count)]
            pltpu.make_async_remote_copy(
                lines, lines, row_send.at[0], recv.at[0], device_id=sibling, device_id_type=MESH
            ).wait_send()


def solution(mesh):
    n_blk = mesh.shape["blk"]

    def on_device(picture_vectors, caption_vectors, positive_partner, inverse_warmth, affine_offset):
        rows, depth = picture_vectors.shape
        out = jax.ShapeDtypeStruct((rows, depth), jnp.bfloat16)
        whole = pl.BlockSpec(memory_space=pl.ANY)
        scalar = pl.BlockSpec(memory_space=pltpu.SMEM)
        local = pl.BlockSpec(memory_space=pltpu.VMEM)
        operands = [
            pltpu.with_memory_space_constraint(operand, pltpu.HBM)
            for operand in (picture_vectors, caption_vectors, positive_partner.reshape(2, 1, rows // 2))
        ]
        return pl.pallas_call(
            functools.partial(kernel, n_blk),
            out_shape=(out, out),
            in_specs=[scalar, scalar, whole, whole, whole],
            out_specs=(local, local),
            scratch_shapes=[
                pltpu.VMEM((2, HOPS, rows, depth), jnp.bfloat16),
                pltpu.VMEM((2, HOPS, 2, 1, rows // 2), jnp.int32),
                pltpu.VMEM((2, rows, 128), jnp.int32),
                pltpu.VMEM((2, rows, depth), jnp.float32),
                pltpu.SemaphoreType.DMA((3,)),
                pltpu.SemaphoreType.DMA((40,)),
                pltpu.SemaphoreType.DMA((1,)),
                pltpu.SemaphoreType.DMA((HOPS - 1,)),
                pltpu.SemaphoreType.DMA((1,)),
            ],
            compiler_params=pltpu.CompilerParams(
                collective_id=0, has_side_effects=True, vmem_limit_bytes=VMEM_LIMIT
            ),
            cost_estimate=pl.CostEstimate(
                flops=64 * rows * rows * depth, bytes_accessed=8 * rows * depth, transcendentals=0
            ),
        )(inverse_warmth, affine_offset, *operands)

    return jax.shard_map(
        on_device,
        mesh=mesh,
        in_specs=(P(("grp", "blk"), None), P(("grp", "blk"), None), P(("grp", "blk")), P(), P()),
        out_specs=(P(("grp", "blk"), None), P(("grp", "blk"), None)),
        check_vma=False,
    )
```

time: 60.2 us -> 53.9 us (0.90)
  Pallas kernels: 53.6 us -> 50.2 us
  local copies, waits for them, and re-layouts: 4.43 us -> 1.63 us
    pallas_call x1, Pallas kernels: 53.6 us -> 50.2 us  [on_device(): pl.pallas_call(functools.partial(kernel, n_blk), out_shape=(out, out), in...]
    unnamed x8 -> x2, local copies, waits for them, and re-layouts: 4.43 us -> 1.63 us
where the time goes in v2:
time: 53.9 us; the launch traced here: 53.8 us
  Pallas kernels  50.2 us (93%)
  between operations  1.93 us (4%)
  local copies, waits for them, and re-layouts  1.63 us (3%)
    pallas_call x1, Pallas kernels, on_device(): pl.pallas_call(functools.partial(kernel, n_blk), out_shape=(out, out), in...  50.2 us
    unnamed x2, local copies, waits for them, and re-layouts  1.63 us

profile of v2, /device:TPU:1, one launch (start us, length us, event | category | flops | bytes accessed | tf_op | source)
XLA Modules:
  0.0 53.8 jit_solution(10208581643894627429)
XLA Ops:
  1.9 50.2 %shard_map.68 = (bf16[256,1152]{1,0:T(8,128)(2,1)S(1)}, bf16[256,1152]{1,0:T(8,128)(2,1)S(1)}) custom-call(f32[1]{0:T(128)S(6)} %copy.9.scale_ref, f32[1]{0:T(128)S(6)} %copy.10.offset_ref, bf16[256,1152]{1,0:T(8,128)(2,1)} %images.1, bf16[256,1152]{1,0:T(8,128)(2,1)} %texts.1, s32[2,1,128]{2,1,0:T(1,128)} %bitcast.1), custom_call_target="tpu_custom_call" | custom-call | flops 4831838208 | bytes 2359296 | tf_op jit(solution)/shard_map/pallas_call | solution.py:253
  52.1 0.8 %copy.11 = bf16[256,1152]{1,0:T(8,128)(2,1)} copy(bf16[256,1152]{1,0:T(8,128)(2,1)S(1)} %get-tuple-element.4) | data formatting | bytes 1179648
  53.0 0.8 %copy.12 = bf16[256,1152]{1,0:T(8,128)(2,1)} copy(bf16[256,1152]{1,0:T(8,128)(2,1)S(1)} %get-tuple-element.5) | data formatting | bytes 1179648

commit v3 on v2

v3 whole, which is shorter than its diff:
```python
import functools

import jax
import jax.numpy as jnp
from jax import lax
from jax.experimental import pallas as pl
from jax.experimental.pallas import tpu as pltpu
from jax.sharding import PartitionSpec as P

MESH = pl.DeviceIdType.MESH
HOPS = 8
TEXT, IMAGE = 0, 1
ASIDE = 32
VMEM_LIMIT = 40 * 2**20


def kernel(
    n_blk, scale_ref, offset_ref, images, texts, labels, image_out, text_out,
    held, rows_of, column_of, total, local_sem, recv, send, row_recv, row_send,
):
    rows = images.shape[0]
    half_rows, part = rows // 2, rows // 4
    n_z = n_blk // 4
    p = lax.axis_index("blk")
    z, x_hi, core = p // 4, (p // 2) % 2, p % 2
    sibling = {"blk": p + 1 - 2 * core}
    partner = {"blk": p + 2 - 4 * x_hi}
    early, late = 1 - x_hi, x_hi
    outer, inner = core, 1 - core
    up = lax.rem(z + 1, n_z) * 4 + p % 4
    down = lax.rem(z + n_z - 1, n_z) * 4 + p % 4

    def along(kind):
        return {"blk": jnp.where(kind == TEXT, up, down)}

    along_early, along_late, along_outer = along(early), along(late), along(outer)

    barrier = pltpu.get_barrier_semaphore()
    for device in (sibling, partner, along_early, along_late):
        pl.semaphore_signal(barrier, inc=1, device_id=device, device_id_type=MESH)
    def load(kind, q):
        span = pl.ds(q * part, part)
        return pltpu.make_async_copy(
            (texts, images)[kind].at[span], held.at[kind, 0, span], local_sem.at[kind * 4 + q]
        )

    load_labels = pltpu.make_async_copy(labels, rows_of.at[IMAGE, 0], local_sem.at[8])
    load_labels.start()
    for q in range(4):
        load(TEXT, q).start()
        load(IMAGE, q).start()
    pl.semaphore_wait(barrier, 4)

    def sem_of(kind, slot, q, is_odd):
        if is_odd:
            return recv.at[24 + kind * 8 + slot // 2 * 2 + q // 2]
        return recv.at[kind * 12 + (slot // 2 - 1) * 4 + q]

    def copy_rows(kind, slot, first, count, to_slot, sem, device, send_sem=0):
        span = pl.ds(first, count)
        return pltpu.make_async_remote_copy(
            src_ref=held.at[kind, slot, span],
            dst_ref=held.at[kind, to_slot, span],
            send_sem=send.at[send_sem],
            recv_sem=sem,
            device_id=device,
            device_id_type=MESH,
        )

    def copy(kind, slot, q, n, to_slot, is_odd, device, send_sem=0):
        sem = sem_of(kind, to_slot, q - q % 2 if is_odd else q, is_odd)
        return copy_rows(kind, slot, q * part, n * part, to_slot, sem, device, send_sem)

    def row_copy(slot, to_slot, device):
        return pltpu.make_async_remote_copy(
            src_ref=rows_of.at[IMAGE, slot],
            dst_ref=rows_of.at[IMAGE, to_slot],
            send_sem=row_send.at[0],
            recv_sem=row_recv.at[to_slot - 1],
            device_id=device,
            device_id_type=MESH,
        )

    def put(kind, slot, q, n, to_slot, is_odd, device, send_sem=0):
        copy(kind, slot, q, n, to_slot, is_odd, device, send_sem).start()
        if q == 0:
            @pl.when(kind == IMAGE)
            def _():
                row_copy(slot, to_slot, device).start()

    def by_z(kind, slot, q, n, to_slot, device):
        put(kind, slot, q, n, to_slot, to_slot == 7, device)

    def by_x(kind, slot, q, n):
        put(kind, slot, q, n, 2, False, partner)

    def by_core(kind, slot, q, n, send_sem=0):
        put(kind, slot, q, n, slot + jnp.where(kind == outer, 1, -1), True, sibling, send_sem)

    aside = rows - ASIDE

    def early_aside(kind):
        return copy_rows(kind, 4, aside, ASIDE, 6, sem_of(kind, 6, 3, False), partner)

    def late_aside(kind):
        return copy_rows(kind, 7, 3 * part, part, 5, recv.at[40], partner)

    def late_aside_on():
        return copy_rows(late, 5, 3 * part, part, 6, sem_of(late, 6, 3, False), sibling, 1)

    def arrived(kind, slot, q, n, is_odd=False):
        copy(kind, slot, q, n, slot, is_odd, sibling).wait_recv()
        if q == 0:
            @pl.when(kind == IMAGE)
            def _():
                row_copy(slot, slot, sibling).wait_recv()

    load(TEXT, 0).wait()
    load(IMAGE, 0).wait()
    load_labels.wait()
    row_copy(0, 4, along(IMAGE)).start()
    pl.when(late == IMAGE)(lambda: row_copy(0, 2, partner).start())
    copy(early, 0, 0, 1, 4, False, along_early).start()
    load(TEXT, 1).wait()
    load(IMAGE, 1).wait()
    copy(late, 0, 0, 2, 4, False, along_late).start()
    copy(late, 0, 0, 2, 2, False, partner).start()
    copy(early, 0, 1, 1, 4, False, along_early).start()
    for q in (2, 3):
        load(TEXT, q).wait()
        load(IMAGE, q).wait()
    copy(early, 0, 2, 1, 4, False, along_early).start()
    copy(late, 0, 2, 2, 4, False, along_late).start()
    copy(late, 0, 2, 2, 2, False, partner).start()
    copy(early, 0, 3, 1, 4, False, along_early).start()
    by_core(outer, 0, 0, 4, 1)

    base = lax.axis_index("grp") * n_blk * rows
    total[...] = jnp.zeros_like(total)
    column_of[IMAGE] = base + p * rows + lax.broadcasted_iota(jnp.int32, (rows, 128), 0)
    for half in range(2):
        column_of[TEXT, pl.ds(half * half_rows, half_rows)] = jnp.transpose(
            jnp.broadcast_to(rows_of[IMAGE, 0, half], (128, half_rows))
        )
        for slot in range(HOPS):
            block = lax.rem(p - slot + n_blk, n_blk)
            rows_of[TEXT, slot, half] = (
                base + block * rows + half * half_rows + lax.broadcasted_iota(jnp.int32, (1, half_rows), 1)
            )

    def first_wave(q):
        arrived(early, 4, q, 1)
        by_x(early, 4, q, 1)
        if q % 2 == 0:
            return
        by_core(early, 4, q - 1, 2)
        arrived(late, 4, q - 1, 2)
        by_core(late, 4, q - 1, 2)
        arrived(early, 2, q - 1, 2)
        if q == 1:
            by_z(early, 2, 0, 2, 6, along_early)
        arrived(outer, 3, q - 1, 2, True)
        if q == 1:
            pl.when(outer == late)(lambda: by_z(outer, 3, 0, 2, 7, along_outer))
        if q == 3:
            by_z(outer, 3, 2, 2, 7, along_outer)
            copy_rows(early, 2, 2 * part, aside - 2 * part, 6, sem_of(early, 6, 2, False), along_early).start()
            pl.when(outer == early)(lambda: by_z(outer, 3, 0, 2, 7, along_outer))
            early_aside(late).start()

    def second_wave(q):
        arrived(late, 2, q, 1)
        if q < 3:
            by_z(late, 2, q, 1, 6, along_late)
        else:
            pl.when(late == outer)(lambda: by_z(late, 2, 3, 1, 6, along_late))
        if q == 1:
            arrived(early, 6, 0, 2)
            by_core(early, 6, 0, 2)
        if q % 2 == 1:
            by_core(late, 2, q - 1, 2)

    def early_end():
        copy_rows(early, 6, 2 * part, aside - 2 * part, 6, sem_of(early, 6, 2, False), sibling).wait_recv()
        early_aside(early).wait_recv()
        by_core(early, 6, 2, 2)

    def last_wave(q):
        arrived(late, 6, q, 1)
        if q == 1:
            by_core(late, 6, 0, 2, 1)
        if q == 2:
            by_core(late, 6, 2, 1, 1)
        if q == 3:
            pl.when(late == outer)(lambda: by_core(late, 6, 3, 1, 1))

    def odd(kind, outer_slot):
        return jnp.where(kind == outer, outer_slot, outer_slot + 2)

    def both(kind, slot):
        return (kind, slot, 0, slot, 1)

    order = [
        (both(early, 0), both(late, 0)),
        (both(early, 2), both(early, 4)),
        (both(late, 4), both(outer, 3)),
        (both(inner, 5), both(inner, 1)),
        (both(early, odd(early, 1)), (late, 2, 0, odd(late, 1), 0)),
        ((early, 6, 0, odd(early, 5), 0), (late, 2, 1, odd(late, 1), 1)),
        ((late, 6, 0, odd(late, 5), 0), (early, 6, 1, odd(early, 5), 1)),
        (both(outer, 7), (late, 6, 1, odd(late, 5), 1)),
    ]

    def write(kind):
        for k, out in enumerate((image_out, text_out)):
            @pl.when(kind == k)
            def _():
                out[...] = total[k].astype(jnp.bfloat16)

    def before(n):
        if n == 1:
            for q in range(4):
                first_wave(q)
            by_core(early, 2, 0, 4)
        if n == 3:
            second_wave(0)
            arrived(inner, 5, 0, 2, True)
            arrived(inner, 5, 2, 2, True)
            arrived(inner, 1, 0, 4, True)
        if n == 4:
            second_wave(1)
            arrived(early, odd(early, 1), 0, 4, True)
            arrived(late, odd(late, 1), 0, 2, True)
        if n == 5:
            second_wave(2)
            last_wave(0)

            @pl.when(outer == early)
            def _():
                arrived(early, 7, 2, 2, True)
                late_aside(early).start()

            second_wave(3)
            last_wave(1)
            arrived(early, odd(early, 5), 0, 2, True)
            arrived(late, odd(late, 1), 2, 2, True)
        if n == 6:
            early_end()
            last_wave(2)

            @pl.when(late == outer)
            def _():
                late_aside(late).wait_recv()
                late_aside_on().start()

            arrived(late, odd(late, 5), 0, 2, True)
            arrived(early, odd(early, 5), 2, 2, True)
        if n == 7:
            last_wave(3)
            arrived(outer, 7, 0, 2, True)
            pl.when(outer == late)(lambda: arrived(outer, 7, 2, 2, True))
            pl.when(late == outer)(lambda: arrived(late, 5, 2, 1, True))
            pl.when(late == inner)(lambda: arrived(late, 7, 2, 2, True))

    scale = scale_ref[0]
    offset = offset_ref[0]

    def multiply(n, carry):
        for step in range(len(order)):
            pl.when(n == step)(functools.partial(before, step))

        def piece(kind, slot, half):
            return held[kind, slot, pl.ds(pl.multiple_of(half * half_rows, half_rows), half_rows)]

        units = []
        for u in range(2):
            picked = list(order[0][u])
            for step in range(1, len(order)):
                for i in range(len(picked)):
                    picked[i] = jnp.where(n == step, order[step][u][i], picked[i])
            kind, slot_a, half_a, slot_b, half_b = picked
            block = jnp.concatenate([piece(kind, slot_a, half_a), piece(kind, slot_b, half_b)], axis=0)
            line = jnp.concatenate([rows_of[kind, slot_a, half_a], rows_of[kind, slot_b, half_b]], axis=1)
            logits = scale * lax.dot_general(
                held[1 - kind, 0], block, (((1,), (1,)), ((), ())), preferred_element_type=jnp.float32
            ) + offset
            units.append((kind, block, line, logits))
        grads = []
        for kind, block, line, logits in units:
            column = jnp.concatenate([column_of[kind]] * (rows // 128), axis=1)
            turn = jnp.where(column == line, -1.0, 1.0)
            coeff = (turn * scale * jax.nn.sigmoid(turn * logits)).astype(jnp.bfloat16)
            grads.append((kind, jnp.dot(coeff, block, preferred_element_type=jnp.float32)))
        for kind, grad in grads:
            total[kind] += grad
        return carry

    lax.fori_loop(0, len(order), multiply, 0)

    write(early)
    write(late)
    def all_sent(refs, send_sem):
        pltpu.make_async_remote_copy(
            refs, refs, send_sem, recv.at[0], device_id=sibling, device_id_type=MESH
        ).wait_send()

    all_sent(held.at[:, pl.ds(0, 6)], send.at[0])
    pl.when(late == outer)(lambda: all_sent(held.at[TEXT, pl.ds(0, 3), pl.ds(0, 3 * part)], send.at[1]))
    pl.when(late == inner)(lambda: all_sent(held.at[TEXT, pl.ds(0, 2), pl.ds(0, rows - part // 2)], send.at[1]))
    for kind, count in ((IMAGE, HOPS), (TEXT, HOPS - 2)):
        @pl.when(outer == kind)
        def _():
            all_sent(rows_of.at[IMAGE, pl.ds(0, count)], row_send.at[0])


def solution(mesh):
    n_blk = mesh.shape["blk"]

    def on_device(picture_vectors, caption_vectors, positive_partner, inverse_warmth, affine_offset):
        rows, depth = picture_vectors.shape
        out = jax.ShapeDtypeStruct((rows, depth), jnp.bfloat16)
        whole = pl.BlockSpec(memory_space=pl.ANY)
        scalar = pl.BlockSpec(memory_space=pltpu.SMEM)
        local = pl.BlockSpec(memory_space=pltpu.VMEM)
        operands = [
            pltpu.with_memory_space_constraint(operand, pltpu.HBM)
            for operand in (picture_vectors, caption_vectors, positive_partner.reshape(2, 1, rows // 2))
        ]
        return pl.pallas_call(
            functools.partial(kernel, n_blk),
            out_shape=(out, out),
            in_specs=[scalar, scalar, whole, whole, whole],
            out_specs=(local, local),
            scratch_shapes=[
                pltpu.VMEM((2, HOPS, rows, depth), jnp.bfloat16),
                pltpu.VMEM((2, HOPS, 2, 1, rows // 2), jnp.int32),
                pltpu.VMEM((2, rows, 128), jnp.int32),
                pltpu.VMEM((2, rows, depth), jnp.float32),
                pltpu.SemaphoreType.DMA((9,)),
                pltpu.SemaphoreType.DMA((41,)),
                pltpu.SemaphoreType.DMA((2,)),
                pltpu.SemaphoreType.DMA((HOPS - 1,)),
                pltpu.SemaphoreType.DMA((1,)),
            ],
            compiler_params=pltpu.CompilerParams(
                collective_id=0, has_side_effects=True, vmem_limit_bytes=VMEM_LIMIT
            ),
            cost_estimate=pl.CostEstimate(
                flops=64 * rows * rows * depth, bytes_accessed=8 * rows * depth, transcendentals=0
            ),
        )(inverse_warmth, affine_offset, *operands)

    return jax.shard_map(
        on_device,
        mesh=mesh,
        in_specs=(P(("grp", "blk"), None), P(("grp", "blk"), None), P(("grp", "blk")), P(), P()),
        out_specs=(P(("grp", "blk"), None), P(("grp", "blk"), None)),
        check_vma=False,
    )
```

time: 53.9 us -> 51.9 us (0.963)
  Pallas kernels: 50.2 us -> 48.1 us
    pallas_call x1, Pallas kernels: 50.2 us -> 48.1 us  [on_device(): pl.pallas_call(functools.partial(kernel, n_blk), out_shape=(out, out), in...]
where the time goes in v3:
time: 51.9 us; the launch traced here: 51.7 us
  Pallas kernels  48.1 us (93%)
  between operations  1.93 us (4%)
  local copies, waits for them, and re-layouts  1.63 us (3%)
    pallas_call x1, Pallas kernels, on_device(): pl.pallas_call(functools.partial(kernel, n_blk), out_shape=(out, out), in...  48.1 us
    unnamed x2, local copies, waits for them, and re-layouts  1.63 us

profile of v3, /device:TPU:1, one launch (start us, length us, event | category | flops | bytes accessed | tf_op | source)
XLA Modules:
  0.0 51.7 jit_solution(8725217532591204459)
XLA Ops:
  1.9 48.1 %shard_map.68 = (bf16[256,1152]{1,0:T(8,128)(2,1)S(1)}, bf16[256,1152]{1,0:T(8,128)(2,1)S(1)}) custom-call(f32[1]{0:T(128)S(6)} %copy.9.scale_ref, f32[1]{0:T(128)S(6)} %copy.10.offset_ref, bf16[256,1152]{1,0:T(8,128)(2,1)} %images.1, bf16[256,1152]{1,0:T(8,128)(2,1)} %texts.1, s32[2,1,128]{2,1,0:T(1,128)} %bitcast.1), custom_call_target="tpu_custom_call" | custom-call | flops 4831838208 | bytes 2359296 | tf_op jit(solution)/shard_map/pallas_call | solution.py:329
  50.1 0.8 %copy.11 = bf16[256,1152]{1,0:T(8,128)(2,1)} copy(bf16[256,1152]{1,0:T(8,128)(2,1)S(1)} %get-tuple-element.4) | data formatting | bytes 1179648
  50.9 0.8 %copy.12 = bf16[256,1152]{1,0:T(8,128)(2,1)} copy(bf16[256,1152]{1,0:T(8,128)(2,1)S(1)} %get-tuple-element.5) | data formatting | bytes 1179648

commit v4 on v3

--- a/solution.py
+++ b/solution.py
@@ -15,8 +15,8 @@
 
 
 def kernel(
-    n_blk, scale_ref, offset_ref, images, texts, labels, image_out, text_out,
-    held, rows_of, column_of, total, local_sem, recv, send, row_recv, row_send,
+    n_blk, scale_ref, offset_ref, images, texts, labels, grads_out,
+    held, rows_of, column_of, total, local_sem, recv, send, row_recv, row_send, ready,
 ):
     rows = images.shape[0]
     half_rows, part = rows // 2, rows // 4
@@ -36,8 +36,15 @@
     along_early, along_late, along_outer = along(early), along(late), along(outer)
 
     barrier = pltpu.get_barrier_semaphore()
-    for device in (sibling, partner, along_early, along_late):
+    for device in (sibling, partner, {"blk": down}):
         pl.semaphore_signal(barrier, inc=1, device_id=device, device_id_type=MESH)
+
+    first, last = z == 0, z == n_z - 1
+
+    @pl.when(jnp.logical_not(last))
+    def _():
+        pl.semaphore_signal(barrier, inc=1, device_id={"blk": up}, device_id_type=MESH)
+
     def load(kind, q):
         span = pl.ds(q * part, part)
         return pltpu.make_async_copy(
@@ -49,7 +56,12 @@
     for q in range(4):
         load(TEXT, q).start()
         load(IMAGE, q).start()
-    pl.semaphore_wait(barrier, 4)
+    pl.semaphore_wait(barrier, jnp.where(first, 3, 4))
+
+    @pl.when(last)
+    def _():
+        pl.semaphore_signal(ready, inc=1, device_id={"blk": up}, device_id_type=MESH)
+
 
     def sem_of(kind, slot, q, is_odd):
         if is_odd:
@@ -100,13 +112,28 @@
     aside = rows - ASIDE
 
     def early_aside(kind):
-        return copy_rows(kind, 4, aside, ASIDE, 6, sem_of(kind, 6, 3, False), partner)
+        return copy_rows(kind, 4, aside, ASIDE, 6, sem_of(kind, 6, 3, False), partner, 2)
+
+    def early_aside_more(kind):
+        return copy_rows(kind, 4, 2 * part, aside - 2 * part, 6, sem_of(kind, 6, 2, False), partner, 2)
+
+    def early_rest():
+        return copy_rows(early, 2, 2 * part, aside - 2 * part, 6, sem_of(early, 6, 2, False), along_early, 2)
 
     def late_aside(kind):
-        return copy_rows(kind, 7, 3 * part, part, 5, recv.at[40], partner)
-
-    def late_aside_on():
-        return copy_rows(late, 5, 3 * part, part, 6, sem_of(late, 6, 3, False), sibling, 1)
+        return copy_rows(kind, 7, 3 * part, part, 5, recv.at[40], partner, 2)
+
+    def late_aside_more(kind):
+        return copy_rows(kind, 7, 2 * part, part, 5, sem_of(kind, 5, 2, True), partner, 2)
+
+    def late_aside_on(q):
+        return copy_rows(late, 5, q * part, part, 6, sem_of(late, 6, q, False), sibling, 1)
+
+    def of_texts(kind, where):
+        return jnp.logical_and(kind == TEXT, where)
+
+    def unless(condition):
+        return pl.when(jnp.logical_not(condition))
 
     def arrived(kind, slot, q, n, is_odd=False):
         copy(kind, slot, q, n, slot, is_odd, sibling).wait_recv()
@@ -115,24 +142,47 @@
             def _():
                 row_copy(slot, slot, sibling).wait_recv()
 
+    def own_by_z(kind, q, n):
+        @pl.when(jnp.logical_or(kind == TEXT, jnp.logical_not(first)))
+        def _():
+            copy(kind, 0, q, n, 4, False, along(kind)).start()
+
+    def own_by_z_at_first():
+        pl.semaphore_wait(ready, 1)
+        row_copy(0, 4, {"blk": down}).start()
+
+        @pl.when(early == IMAGE)
+        def _():
+            for q in range(4):
+                copy(IMAGE, 0, q, 1, 4, False, {"blk": down}).start()
+
+        @pl.when(late == IMAGE)
+        def _():
+            for q in (0, 2):
+                copy(IMAGE, 0, q, 2, 4, False, {"blk": down}).start()
+
     load(TEXT, 0).wait()
     load(IMAGE, 0).wait()
     load_labels.wait()
-    row_copy(0, 4, along(IMAGE)).start()
+    pl.when(jnp.logical_not(first))(lambda: row_copy(0, 4, {"blk": down}).start())
     pl.when(late == IMAGE)(lambda: row_copy(0, 2, partner).start())
-    copy(early, 0, 0, 1, 4, False, along_early).start()
+    own_by_z(early, 0, 1)
     load(TEXT, 1).wait()
     load(IMAGE, 1).wait()
-    copy(late, 0, 0, 2, 4, False, along_late).start()
+    own_by_z(late, 0, 2)
     copy(late, 0, 0, 2, 2, False, partner).start()
-    copy(early, 0, 1, 1, 4, False, along_early).start()
+    own_by_z(early, 1, 1)
     for q in (2, 3):
         load(TEXT, q).wait()
         load(IMAGE, q).wait()
-    copy(early, 0, 2, 1, 4, False, along_early).start()
-    copy(late, 0, 2, 2, 4, False, along_late).start()
-    copy(late, 0, 2, 2, 2, False, partner).start()
-    copy(early, 0, 3, 1, 4, False, along_early).start()
+    own_by_z(early, 2, 1)
+    own_by_z(late, 2, 2)
+
+    def own_by_x_rest():
+        copy(late, 0, 2, 2, 2, False, partner).start()
+
+    pl.when(jnp.logical_not(jnp.logical_and(last, late == IMAGE)))(own_by_x_rest)
+    own_by_z(early, 3, 1)
     by_core(outer, 0, 0, 4, 1)
 
     base = lax.axis_index("grp") * n_blk * rows
@@ -148,32 +198,101 @@
                 base + block * rows + half * half_rows + lax.broadcasted_iota(jnp.int32, (1, half_rows), 1)
             )
 
-    def first_wave(q):
+    def early_four(q):
         arrived(early, 4, q, 1)
         by_x(early, 4, q, 1)
-        if q % 2 == 0:
-            return
-        by_core(early, 4, q - 1, 2)
+        if q % 2 == 1:
+            by_core(early, 4, q - 1, 2)
+
+    def late_four(q):
         arrived(late, 4, q - 1, 2)
         by_core(late, 4, q - 1, 2)
+
+    def early_two(q):
         arrived(early, 2, q - 1, 2)
         if q == 1:
             by_z(early, 2, 0, 2, 6, along_early)
+
+    def outer_three(q):
         arrived(outer, 3, q - 1, 2, True)
         if q == 1:
             pl.when(outer == late)(lambda: by_z(outer, 3, 0, 2, 7, along_outer))
         if q == 3:
             by_z(outer, 3, 2, 2, 7, along_outer)
-            copy_rows(early, 2, 2 * part, aside - 2 * part, 6, sem_of(early, 6, 2, False), along_early).start()
-            pl.when(outer == early)(lambda: by_z(outer, 3, 0, 2, 7, along_outer))
-            early_aside(late).start()
+
+    def early_two_rest():
+        unless(of_texts(early, last))(lambda: early_rest().start())
+        pl.when(outer == early)(lambda: by_z(outer, 3, 0, 2, 7, along_outer))
+
+    def late_four_aside():
+        pl.when(of_texts(late, first))(lambda: early_aside_more(late).start())
+        early_aside(late).start()
+
+    def first_wave():
+        @unless(last)
+        def _():
+            for q in range(4):
+                early_four(q)
+                if q % 2 == 1:
+                    late_four(q)
+                    early_two(q)
+                    outer_three(q)
+            early_two_rest()
+            late_four_aside()
+
+        @pl.when(jnp.logical_and(last, early == TEXT))
+        def _():
+            for q in range(4):
+                early_four(q)
+                if q == 3:
+                    own_by_x_rest()
+                if q % 2 == 1:
+                    early_two(q)
+                    pl.when(outer == early)(lambda: outer_three(q))
+            pl.when(outer == early)(early_two_rest)
+            late_four(1)
+            late_four(3)
+            late_four_aside()
+
+            @pl.when(outer == late)
+            def _():
+                outer_three(1)
+                outer_three(3)
+                early_two_rest()
+
+        @pl.when(jnp.logical_and(last, late == TEXT))
+        def _():
+            early_four(0)
+            late_four(1)
+            pl.when(outer == late)(lambda: outer_three(1))
+            early_four(1)
+            late_two(0)
+            early_two(1)
+            pl.when(outer == early)(lambda: outer_three(1))
+            late_four(3)
+            late_two(1)
+            early_four(2)
+            early_four(3)
+            late_two(2)
+            late_two(3)
+            outer_three(3)
+            early_two(3)
+            early_two_rest()
+            late_four_aside()
+
+    def late_two(q):
+        arrived(late, 2, q, 1)
+        if q < 2:
+            by_z(late, 2, q, 1, 6, along_late)
+        if q == 2:
+            unless(jnp.logical_and(late == inner, of_texts(late, last)))(
+                lambda: copy(late, 2, 2, 1, 6, False, along_late, 2).start()
+            )
+        if q == 3:
+            pl.when(late == outer)(lambda: copy(late, 2, 3, 1, 6, False, along_late, 2).start())
 
     def second_wave(q):
-        arrived(late, 2, q, 1)
-        if q < 3:
-            by_z(late, 2, q, 1, 6, along_late)
-        else:
-            pl.when(late == outer)(lambda: by_z(late, 2, 3, 1, 6, along_late))
+        unless(jnp.logical_and(last, late == TEXT))(lambda: late_two(q))
         if q == 1:
             arrived(early, 6, 0, 2)
             by_core(early, 6, 0, 2)
@@ -190,7 +309,7 @@
         if q == 1:
             by_core(late, 6, 0, 2, 1)
         if q == 2:
-            by_core(late, 6, 2, 1, 1)
+            unless(jnp.logical_and(late == inner, of_texts(late, first)))(lambda: by_core(late, 6, 2, 1, 1))
         if q == 3:
             pl.when(late == outer)(lambda: by_core(late, 6, 3, 1, 1))
 
@@ -211,19 +330,14 @@
         (both(outer, 7), (late, 6, 1, odd(late, 5), 1)),
     ]
 
-    def write(kind):
-        for k, out in enumerate((image_out, text_out)):
-            @pl.when(kind == k)
-            def _():
-                out[...] = total[k].astype(jnp.bfloat16)
-
     def before(n):
         if n == 1:
-            for q in range(4):
-                first_wave(q)
+            pl.when(first)(own_by_z_at_first)
+            first_wave()
             by_core(early, 2, 0, 4)
+        if n == 2:
+            second_wave(0)
         if n == 3:
-            second_wave(0)
             arrived(inner, 5, 0, 2, True)
             arrived(inner, 5, 2, 2, True)
             arrived(inner, 1, 0, 4, True)
@@ -239,6 +353,7 @@
             def _():
                 arrived(early, 7, 2, 2, True)
                 late_aside(early).start()
+                pl.when(of_texts(early, first))(lambda: late_aside_more(early).start())
 
             second_wave(3)
             last_wave(1)
@@ -251,7 +366,12 @@
             @pl.when(late == outer)
             def _():
                 late_aside(late).wait_recv()
-                late_aside_on().start()
+                late_aside_on(3).start()
+
+                @pl.when(of_texts(late, first))
+                def _():
+                    arrived(late, 5, 2, 1, True)
+                    late_aside_on(2).start()
 
             arrived(late, odd(late, 5), 0, 2, True)
             arrived(early, odd(early, 5), 2, 2, True)
@@ -259,7 +379,9 @@
             last_wave(3)
             arrived(outer, 7, 0, 2, True)
             pl.when(outer == late)(lambda: arrived(outer, 7, 2, 2, True))
-            pl.when(late == outer)(lambda: arrived(late, 5, 2, 1, True))
+            pl.when(jnp.logical_and(late == outer, jnp.logical_not(of_texts(late, first))))(
+                lambda: arrived(late, 5, 2, 1, True)
+            )
             pl.when(late == inner)(lambda: arrived(late, 7, 2, 2, True))
 
     scale = scale_ref[0]
@@ -297,16 +419,39 @@
 
     lax.fori_loop(0, len(order), multiply, 0)
 
-    write(early)
-    write(late)
+    grads_out[...] = total[...].astype(jnp.bfloat16)
     def all_sent(refs, send_sem):
         pltpu.make_async_remote_copy(
             refs, refs, send_sem, recv.at[0], device_id=sibling, device_id_type=MESH
         ).wait_send()
 
-    all_sent(held.at[:, pl.ds(0, 6)], send.at[0])
-    pl.when(late == outer)(lambda: all_sent(held.at[TEXT, pl.ds(0, 3), pl.ds(0, 3 * part)], send.at[1]))
-    pl.when(late == inner)(lambda: all_sent(held.at[TEXT, pl.ds(0, 2), pl.ds(0, rows - part // 2)], send.at[1]))
+    def rows_sent(count, send_sem, also):
+        parts = next(n for n in range(1, HOPS) if count % (16 * n) == 0 and count <= rows * n)
+
+        @pl.when(also)
+        def _():
+            all_sent(held.at[TEXT, pl.ds(0, parts), pl.ds(0, count // parts)], send.at[send_sem])
+
+    all_sent(held.at[:, :, pl.ds(0, 11 * part // 4)], send.at[0])
+    late_outer, late_inner = late == outer, late == inner
+    more, fewer = of_texts(late, first), of_texts(late, first)
+    rows_sent(9 * part, 1, jnp.logical_and(late_outer, jnp.logical_not(more)))
+    rows_sent(10 * part, 1, jnp.logical_and(late_outer, more))
+    rows_sent(7 * part, 1, jnp.logical_and(late_inner, jnp.logical_not(fewer)))
+    rows_sent(6 * part, 1, jnp.logical_and(late_inner, fewer))
+    rest = aside - 2 * part
+    texts_late = late == TEXT
+    changes = [
+        (-rest, jnp.logical_and(last, jnp.logical_not(texts_late))),
+        (-part, jnp.logical_and(jnp.logical_and(last, texts_late), late_inner)),
+        (rest, jnp.logical_and(first, texts_late)),
+        (part, jnp.logical_and(jnp.logical_and(first, jnp.logical_not(texts_late)), early == outer)),
+    ]
+    usual = jnp.bool_(True)
+    for change, where in changes:
+        rows_sent(4 * part + change, 2, where)
+        usual = jnp.logical_and(usual, jnp.logical_not(where))
+    rows_sent(4 * part, 2, usual)
     for kind, count in ((IMAGE, HOPS), (TEXT, HOPS - 2)):
         @pl.when(outer == kind)
         def _():
@@ -318,7 +463,6 @@
 
     def on_device(picture_vectors, caption_vectors, positive_partner, inverse_warmth, affine_offset):
         rows, depth = picture_vectors.shape
-        out = jax.ShapeDtypeStruct((rows, depth), jnp.bfloat16)
         whole = pl.BlockSpec(memory_space=pl.ANY)
         scalar = pl.BlockSpec(memory_space=pltpu.SMEM)
         local = pl.BlockSpec(memory_space=pltpu.VMEM)
@@ -326,11 +470,11 @@
             pltpu.with_memory_space_constraint(operand, pltpu.HBM)
             for operand in (picture_vectors, caption_vectors, positive_partner.reshape(2, 1, rows // 2))
         ]
-        return pl.pallas_call(
+        grads = pl.pallas_call(
             functools.partial(kernel, n_blk),
-            out_shape=(out, out),
+            out_shape=jax.ShapeDtypeStruct((2, rows, depth), jnp.bfloat16),
             in_specs=[scalar, scalar, whole, whole, whole],
-            out_specs=(local, local),
+            out_specs=local,
             scratch_shapes=[
                 pltpu.VMEM((2, HOPS, rows, depth), jnp.bfloat16),
                 pltpu.VMEM((2, HOPS, 2, 1, rows // 2), jnp.int32),
@@ -338,9 +482,10 @@
                 pltpu.VMEM((2, rows, depth), jnp.float32),
                 pltpu.SemaphoreType.DMA((9,)),
                 pltpu.SemaphoreType.DMA((41,)),
-                pltpu.SemaphoreType.DMA((2,)),
+                pltpu.SemaphoreType.DMA((3,)),
                 pltpu.SemaphoreType.DMA((HOPS - 1,)),
                 pltpu.SemaphoreType.DMA((1,)),
+                pltpu.SemaphoreType.REGULAR,
             ],
             compiler_params=pltpu.CompilerParams(
                 collective_id=0, has_side_effects=True, vmem_limit_bytes=VMEM_LIMIT
@@ -349,6 +494,7 @@
                 flops=64 * rows * rows * depth, bytes_accessed=8 * rows * depth, transcendentals=0
             ),
         )(inverse_warmth, affine_offset, *operands)
+        return grads[TEXT], grads[IMAGE]
 
     return jax.shard_map(
         on_device,

time: 51.9 us -> 49.7 us (0.958)
  Pallas kernels: 48.1 us -> 46.5 us
  local copies, waits for them, and re-layouts: 1.63 us -> 1.1 us
    pallas_call x1, Pallas kernels: 48.1 us -> 46.5 us  [on_device(): pl.pallas_call(functools.partial(kernel, n_blk), out_shape=jax.ShapeDtype...]
    unnamed x2 -> x0, local copies, waits for them, and re-layouts: 1.63 us -> none
    squeeze x0 -> x1, local copies, waits for them, and re-layouts: none -> 1.1 us  [on_device(): return (grads[TEXT], grads[IMAGE])]
where the time goes in v4:
time: 49.7 us; the launch traced here: 49.5 us
  Pallas kernels  46.5 us (94%)
  between operations  1.93 us (4%)
  local copies, waits for them, and re-layouts  1.1 us (2%)
    pallas_call x1, Pallas kernels, on_device(): pl.pallas_call(functools.partial(kernel, n_blk), out_shape=jax.ShapeDtype...  46.5 us
    squeeze x1, local copies, waits for them, and re-layouts, on_device(): return (grads[TEXT], grads[IMAGE])  1.1 us

profile of v4, /device:TPU:1, one launch (start us, length us, event | category | flops | bytes accessed | tf_op | source)
XLA Modules:
  0.0 49.5 jit_solution(277379873349385364)
XLA Ops:
  1.9 46.5 %shard_map.68 = bf16[2,256,1152]{2,1,0:T(8,128)(2,1)S(1)} custom-call(f32[1]{0:T(128)S(6)} %copy.7.scale_ref, f32[1]{0:T(128)S(6)} %copy.8.offset_ref, bf16[256,1152]{1,0:T(8,128)(2,1)} %images.1, bf16[256,1152]{1,0:T(8,128)(2,1)} %texts.1, s32[2,1,128]{2,1,0:T(1,128)} %bitcast.5), custom_call_target="tpu_custom_call" | custom-call | flops 4831838208 | bytes 2359296 | tf_op jit(solution)/shard_map/pallas_call | solution.py:473
  48.4 1.1 %slice_bitcast_fusion = (bf16[256,1152]{1,0:T(8,128)(2,1)}, bf16[256,1152]{1,0:T(8,128)(2,1)}) fusion(bf16[2,256,1152]{2,1,0:T(8,128)(2,1)S(1)} %shard_map.68), kind=kLoop, calls=%fused_computation | loop fusion | bytes 2359296 | tf_op jit(solution)/shard_map/squeeze | solution.py:497

commit v5 on v4

--- a/solution.py
+++ b/solution.py
@@ -35,16 +35,6 @@
 
     along_early, along_late, along_outer = along(early), along(late), along(outer)
 
-    barrier = pltpu.get_barrier_semaphore()
-    for device in (sibling, partner, {"blk": down}):
-        pl.semaphore_signal(barrier, inc=1, device_id=device, device_id_type=MESH)
-
-    first, last = z == 0, z == n_z - 1
-
-    @pl.when(jnp.logical_not(last))
-    def _():
-        pl.semaphore_signal(barrier, inc=1, device_id={"blk": up}, device_id_type=MESH)
-
     def load(kind, q):
         span = pl.ds(q * part, part)
         return pltpu.make_async_copy(
@@ -52,8 +42,20 @@
         )
 
     load_labels = pltpu.make_async_copy(labels, rows_of.at[IMAGE, 0], local_sem.at[8])
+    load(TEXT, 0).start()
+    load(IMAGE, 0).start()
+    barrier = pltpu.get_barrier_semaphore()
+    for device in (sibling, partner, {"blk": down}):
+        pl.semaphore_signal(barrier, inc=1, device_id=device, device_id_type=MESH)
+
+    first, last = z == 0, z == n_z - 1
+
+    @pl.when(jnp.logical_not(last))
+    def _():
+        pl.semaphore_signal(barrier, inc=1, device_id={"blk": up}, device_id_type=MESH)
+
     load_labels.start()
-    for q in range(4):
+    for q in range(1, 4):
         load(TEXT, q).start()
         load(IMAGE, q).start()
     pl.semaphore_wait(barrier, jnp.where(first, 3, 4))
@@ -163,10 +165,10 @@
 
     load(TEXT, 0).wait()
     load(IMAGE, 0).wait()
+    own_by_z(early, 0, 1)
     load_labels.wait()
     pl.when(jnp.logical_not(first))(lambda: row_copy(0, 4, {"blk": down}).start())
     pl.when(late == IMAGE)(lambda: row_copy(0, 2, partner).start())
-    own_by_z(early, 0, 1)
     load(TEXT, 1).wait()
     load(IMAGE, 1).wait()
     own_by_z(late, 0, 2)
@@ -361,21 +363,24 @@
             arrived(late, odd(late, 1), 2, 2, True)
         if n == 6:
             early_end()
-            last_wave(2)
-
-            @pl.when(late == outer)
+            unless(jnp.logical_and(late == inner, of_texts(late, first)))(lambda: last_wave(2))
+
+            @pl.when(jnp.logical_and(late == outer, jnp.logical_not(of_texts(late, first))))
             def _():
                 late_aside(late).wait_recv()
                 late_aside_on(3).start()
 
-                @pl.when(of_texts(late, first))
-                def _():
-                    arrived(late, 5, 2, 1, True)
-                    late_aside_on(2).start()
-
             arrived(late, odd(late, 5), 0, 2, True)
             arrived(early, odd(early, 5), 2, 2, True)
         if n == 7:
+            @pl.when(jnp.logical_and(late == outer, of_texts(late, first)))
+            def _():
+                late_aside(late).wait_recv()
+                late_aside_on(3).start()
+                arrived(late, 5, 2, 1, True)
+                late_aside_on(2).start()
+
+            pl.when(jnp.logical_and(late == inner, of_texts(late, first)))(lambda: last_wave(2))
             last_wave(3)
             arrived(outer, 7, 0, 2, True)
             pl.when(outer == late)(lambda: arrived(outer, 7, 2, 2, True))

time: 49.7 us -> 49.4 us (level); the launches traced: 49.5 us -> 48.5 us
  Pallas kernels: 46.5 us -> 45.5 us
    pallas_call x1, Pallas kernels: 46.5 us -> 45.5 us  [on_device(): pl.pallas_call(functools.partial(kernel, n_blk), out_shape=jax.ShapeDtype...]
where the time goes in v5:
time: 49.4 us; the launch traced here: 48.5 us
  Pallas kernels  45.5 us (92%)
  between operations  1.93 us (4%)
  local copies, waits for them, and re-layouts  1.1 us (2%)
    pallas_call x1, Pallas kernels, on_device(): pl.pallas_call(functools.partial(kernel, n_blk), out_shape=jax.ShapeDtype...  45.5 us
    squeeze x1, local copies, waits for them, and re-layouts, on_device(): return (grads[TEXT], grads[IMAGE])  1.1 us

profile of v5, /device:TPU:1, one launch (start us, length us, event | category | flops | bytes accessed | tf_op | source)
XLA Modules:
  0.0 48.5 jit_solution(16363942584724363785)
XLA Ops:
  1.9 45.5 %shard_map.68 = bf16[2,256,1152]{2,1,0:T(8,128)(2,1)S(1)} custom-call(f32[1]{0:T(128)S(6)} %copy.7.scale_ref, f32[1]{0:T(128)S(6)} %copy.8.offset_ref, bf16[256,1152]{1,0:T(8,128)(2,1)} %images.1, bf16[256,1152]{1,0:T(8,128)(2,1)} %texts.1, s32[2,1,128]{2,1,0:T(1,128)} %bitcast.5), custom_call_target="tpu_custom_call" | custom-call | flops 4831838208 | bytes 2359296 | tf_op jit(solution)/shard_map/pallas_call | solution.py:478
  47.4 1.1 %slice_bitcast_fusion = (bf16[256,1152]{1,0:T(8,128)(2,1)}, bf16[256,1152]{1,0:T(8,128)(2,1)}) fusion(bf16[2,256,1152]{2,1,0:T(8,128)(2,1)S(1)} %shard_map.68), kind=kLoop, calls=%fused_computation | loop fusion | bytes 2359296 | tf_op jit(solution)/shard_map/squeeze | solution.py:502

commit v6 on v5

--- a/solution.py
+++ b/solution.py
@@ -392,39 +392,57 @@
     scale = scale_ref[0]
     offset = offset_ref[0]
 
+    def coefficients(picked):
+        kind, slot_a, half_a, slot_b, half_b = picked
+
+        def piece(slot, half):
+            return held[kind, slot, pl.ds(pl.multiple_of(half * half_rows, half_rows), half_rows)]
+
+        block = jnp.concatenate([piece(slot_a, half_a), piece(slot_b, half_b)], axis=0)
+        line = jnp.concatenate([rows_of[kind, slot_a, half_a], rows_of[kind, slot_b, half_b]], axis=1)
+        logits = scale * lax.dot_general(
+            held[1 - kind, 0], block, (((1,), (1,)), ((), ())), preferred_element_type=jnp.float32
+        ) + offset
+        column = jnp.concatenate([column_of[kind]] * (rows // 128), axis=1)
+        turn = jnp.where(column == line, -1.0, 1.0)
+        return (turn * scale * jax.nn.sigmoid(turn * logits)).astype(jnp.bfloat16), block
+
+    def product(coeff, block):
+        return jnp.dot(coeff, block, preferred_element_type=jnp.float32)
+
     def multiply(n, carry):
-        for step in range(len(order)):
+        for step in range(len(order) - 1):
             pl.when(n == step)(functools.partial(before, step))
-
-        def piece(kind, slot, half):
-            return held[kind, slot, pl.ds(pl.multiple_of(half * half_rows, half_rows), half_rows)]
-
         units = []
         for u in range(2):
             picked = list(order[0][u])
-            for step in range(1, len(order)):
+            for step in range(1, len(order) - 1):
                 for i in range(len(picked)):
                     picked[i] = jnp.where(n == step, order[step][u][i], picked[i])
-            kind, slot_a, half_a, slot_b, half_b = picked
-            block = jnp.concatenate([piece(kind, slot_a, half_a), piece(kind, slot_b, half_b)], axis=0)
-            line = jnp.concatenate([rows_of[kind, slot_a, half_a], rows_of[kind, slot_b, half_b]], axis=1)
-            logits = scale * lax.dot_general(
-                held[1 - kind, 0], block, (((1,), (1,)), ((), ())), preferred_element_type=jnp.float32
-            ) + offset
-            units.append((kind, block, line, logits))
-        grads = []
-        for kind, block, line, logits in units:
-            column = jnp.concatenate([column_of[kind]] * (rows // 128), axis=1)
-            turn = jnp.where(column == line, -1.0, 1.0)
-            coeff = (turn * scale * jax.nn.sigmoid(turn * logits)).astype(jnp.bfloat16)
-            grads.append((kind, jnp.dot(coeff, block, preferred_element_type=jnp.float32)))
+            units.append((picked[0], coefficients(picked)))
+        grads = [(kind, product(*unit)) for kind, unit in units]
         for kind, grad in grads:
             total[kind] += grad
         return carry
 
-    lax.fori_loop(0, len(order), multiply, 0)
-
-    grads_out[...] = total[...].astype(jnp.bfloat16)
+    lax.fori_loop(0, len(order) - 1, multiply, 0)
+
+    @pl.when(outer == late)
+    def _():
+        grads_out[early] = total[early].astype(jnp.bfloat16)
+
+    before(len(order) - 1)
+    unit_a, unit_b = [coefficients(picked) for picked in order[-1]]
+
+    @pl.when(outer == late)
+    def _():
+        grads_out[late] = (total[late] + product(*unit_a) + product(*unit_b)).astype(jnp.bfloat16)
+
+    @pl.when(outer == early)
+    def _():
+        grads_out[early] = (total[early] + product(*unit_a)).astype(jnp.bfloat16)
+        grads_out[late] = (total[late] + product(*unit_b)).astype(jnp.bfloat16)
+
     def all_sent(refs, send_sem):
         pltpu.make_async_remote_copy(
             refs, refs, send_sem, recv.at[0], device_id=sibling, device_id_type=MESH

time: 49.4 us -> 49.4 us (level)
  no operation moved by 1% of the time
where the time goes in v6:
time: 49.4 us; the launch traced here: 48.5 us
  Pallas kernels  45.5 us (92%)
  between operations  1.93 us (4%)
  local copies, waits for them, and re-layouts  1.1 us (2%)
    pallas_call x1, Pallas kernels, on_device(): pl.pallas_call(functools.partial(kernel, n_blk), out_shape=jax.ShapeDtype...  45.5 us
    squeeze x1, local copies, waits for them, and re-layouts, on_device(): return (grads[TEXT], grads[IMAGE])  1.1 us

profile of v6, /device:TPU:1, one launch (start us, length us, event | category | flops | bytes accessed | tf_op | source)
XLA Modules:
  0.0 48.5 jit_solution(16104916371732805138)
XLA Ops:
  1.9 45.5 %shard_map.68 = bf16[2,256,1152]{2,1,0:T(8,128)(2,1)S(1)} custom-call(f32[1]{0:T(128)S(6)} %copy.7.scale_ref, f32[1]{0:T(128)S(6)} %copy.8.offset_ref, bf16[256,1152]{1,0:T(8,128)(2,1)} %images.1, bf16[256,1152]{1,0:T(8,128)(2,1)} %texts.1, s32[2,1,128]{2,1,0:T(1,128)} %bitcast.5), custom_call_target="tpu_custom_call" | custom-call | flops 4831838208 | bytes 2359296 | tf_op jit(solution)/shard_map/pallas_call | solution.py:496
  47.4 1.1 %slice_bitcast_fusion = (bf16[256,1152]{1,0:T(8,128)(2,1)}, bf16[256,1152]{1,0:T(8,128)(2,1)}) fusion(bf16[2,256,1152]{2,1,0:T(8,128)(2,1)S(1)} %shard_map.68), kind=kLoop, calls=%fused_computation | loop fusion | bytes 2359296 | tf_op jit(solution)/shard_map/squeeze | solution.py:520
